TPU v7x, 32 devices: a whole 2x2x4 slice. The times are simulated.
32 devices in a mesh: rep: 16 (over z, x, core), exp: 2 (over y).
Axes of the slice: x: 2, y: 2, z: 4, core: 2. Of those that a mesh axis runs over, the one named last changes fastest.
Arguments:
- tokens: bfloat16 [25216, 384], P(('rep', 'exp')), may hold values from -6 to 6
- routes: int32 [25216, 2], P(('rep', 'exp')), may hold values from 0 to 7, all different within a row; in each aligned block of 788 rows (0 to 787, 788 to 1575, ...) at most 394 rows name the same one
- norm_gains: float32 [4, 384], replicated, may hold values from 0.25 to 1.75
- attn_qkv: bfloat16 [2, 384, 1152], replicated, may hold values from -0.3125 to 0.3125
- attn_out: bfloat16 [2, 384, 384], replicated, may hold values from -1.75 to 1.75
- mlp_in: bfloat16 [384, 1536], replicated, may hold values from -0.3125 to 0.3125
- mlp_out: bfloat16 [1536, 384], replicated, may hold values from -0.3125 to 0.3125
- router: bfloat16 [384, 8], replicated, may hold values from -0.21875 to 0.21875
- experts_in: bfloat16 [8, 384, 1536], P('exp'), may hold values from -0.3125 to 0.3125
- experts_out: bfloat16 [8, 1536, 384], P('exp'), may hold values from -0.3125 to 0.3125
- cotangent: bfloat16 [25216, 384], P(('rep', 'exp')), may hold values from -6 to 6
Outputs:
- activations: bfloat16 [25216, 384], P(('rep', 'exp'))
- input_grad: float32 [25216, 384], P(('rep', 'exp'))
- qkv_grad: float32 [2, 384, 1152], replicated
- proj_grad: float32 [2, 384, 384], replicated
- gain_grad: float32 [4, 384], replicated
- mlp_in_grad: float32 [384, 1536], replicated
- mlp_out_grad: float32 [1536, 384], replicated
- router_grad: float32 [384, 8], replicated
- experts_in_grad: float32 [8, 384, 1536], P('exp', None, 'rep')
- experts_out_grad: float32 [8, 1536, 384], P('exp', 'rep')
Inputs may be any that keep to these rules, and one draw needn't show every extreme that they name: `routes`: each row names 2 different experts; of the 788 rows of one device no expert is named by more than 394 rows, and in every draw some expert is named by exactly 394 rows of some device.
All inputs are finite; a program needn't handle non-finite values.
Results may differ from a plain program's by a relative error of at most 0.025.
Values may be sent and summed in bfloat16 or wider, within the bound.
A program may use at most 320 MiB of HBM per device.

v0:
```python
import functools
import math

import jax
import jax.numpy as jnp
from jax import lax
from jax.experimental import pallas as pl
from jax.experimental.pallas import tpu as pltpu
from jax.sharding import PartitionSpec as P

F32 = jnp.float32
BF = jnp.bfloat16
HEADS = 6
PATCHES = 197
ROWS = 208
EPS = 1e-6
TILE = 256
D = 384
FF = 1536
VMEM = pl.BlockSpec(memory_space=pltpu.VMEM)


def dot(a, b):
    return lax.dot_general(a, b, (((1,), (0,)), ((), ())), preferred_element_type=F32)


def dot_t(a, b):
    return lax.dot_general(a, b, (((1,), (1,)), ((), ())), preferred_element_type=F32)


def t_dot(a, b):
    return lax.dot_general(a, b, (((0,), (0,)), ((), ())), preferred_element_type=F32)


def norm_parts(x):
    centred = x - jnp.mean(x, axis=-1, keepdims=True)
    rstd = lax.rsqrt(jnp.mean(centred * centred, axis=-1, keepdims=True) + EPS)
    return centred * rstd, rstd


def norm_back(grad, x, gain):
    xh, rstd = norm_parts(x)
    dxh = grad * gain
    inner = dxh - jnp.mean(dxh, axis=-1, keepdims=True)
    return rstd * (inner - xh * jnp.mean(dxh * xh, axis=-1, keepdims=True)), grad * xh


def gelu_parts(h):
    phi = 0.5 + 0.5 * lax.erf(0.7071067811865476 * h)
    e = jnp.exp2(h * h * -0.7213475204444817)
    return h * phi, phi + h * (0.3989422804014327 * e)


def lane_low(rows):
    return lax.broadcasted_iota(jnp.int32, (rows, 128), 1) < 64


MESH = pl.DeviceIdType.MESH
BITS = "cyxhl"


class Place:
    def __init__(self):
        r = lax.axis_index("rep")
        y = lax.axis_index("exp")
        self.bit = {"c": r % 2, "y": y, "x": (r // 2) % 2, "h": r // 8, "l": (r // 4) % 2}
        stride = {"c": 1, "x": 2, "l": 4, "h": 8}
        self.partner = {b: (r + stride[b] * (1 - 2 * self.bit[b]), y) for b in stride}
        self.partner["y"] = (r, 1 - y)
        self.others = []
        for k in range(1, 4):
            z = (r // 4 + k) % 4
            self.others.append(({"h": z // 2, "l": z % 2}, (z * 4 + r % 4, y)))

    def meet(self, partners):
        barrier = pltpu.get_barrier_semaphore()
        for partner in partners:
            pl.semaphore_signal(barrier, inc=1, device_id=partner, device_id_type=MESH)
        pl.semaphore_wait(barrier, len(partners))


class Links:
    def __init__(self, send, recv):
        self.send, self.recv, self.used = send, recv, 0

    def reserve(self, count):
        first = self.used
        self.used += count
        return first

    def copy(self, at, src, dst, device):
        return pltpu.make_async_remote_copy(
            src_ref=src, dst_ref=dst, send_sem=self.send.at[at], recv_sem=self.recv.at[at],
            device_id=device, device_id_type=MESH,
        )

    def start(self, at, src, dst, device):
        copy = self.copy(at, src, dst, device)
        copy.start()
        return copy


def fwd_kernel(linked, *refs):
    names = ["tokens", "cot", "routes", "gains", "wqkv", "wo", "win", "wout"]
    names += ["x0", "cot_out", "x1", "x2", "x3", "qkv1", "qkv2", "o1", "o2", "p1", "p2", "u", "gp", "c"]
    if linked:
        names += ["c_rx", "cot_rx", "routes_rx"]
    names += ["wide"]
    if linked:
        names += ["c_scr", "send", "recv"]
    r = dict(zip(names, refs, strict=True))
    gains = r["gains"]
    ib = r["x1"].shape[0]
    m = ib * ROWS
    images = r["x0"].shape[0]
    step = pl.program_id(0)
    lo = lane_low(ROWS)
    valid = lax.broadcasted_iota(jnp.int32, (ROWS, ROWS), 1) < PATCHES
    real = lax.broadcasted_iota(jnp.int32, (ROWS, D), 0) < PATCHES
    if linked:
        place = Place()
        links = Links(r["send"], r["recv"])

        def exchange(at, src, dst):
            return links.copy(at, src, dst, place.partner["y"])

        early = [exchange(0, r["cot_out"], r["cot_rx"]), exchange(1, r["routes"], r["routes_rx"])]

        def c_copy(image):
            return exchange(2 + image, r["c_scr"].at[image], r["c_rx"].at[image])

    @pl.when(step == 0)
    def _():
        wide = r["wide"]
        for source, target in (("tokens", "x0"), ("cot", "cot_out")):
            wide[0 : images * PATCHES] = r[source][...].astype(F32)
            for i in range(images):
                rows = wide[i * PATCHES : i * PATCHES + ROWS]
                r[target][i] = jnp.where(real, rows, 0.0).astype(BF)
        if linked:
            place.meet([place.partner["y"]])
            for copy in early:
                copy.start()

    def attend_image(i, qkv_ref, o_ref, p_ref):
        for pair in range(HEADS // 2):
            at = 128 * pair
            q = qkv_ref[i, :, at : at + 128] * BF(0.125)
            k = qkv_ref[i, :, D + at : D + at + 128]
            w = qkv_ref[i, :, 2 * D + at : 2 * D + at + 128]
            mixed = []
            for h in range(2):
                qm = jnp.where(lo if h == 0 else ~lo, q, BF(0))
                s = jnp.where(valid, dot_t(qm, k), -1e30)
                s = jnp.exp(s - jnp.max(s, axis=-1, keepdims=True))
                p = (s * (1.0 / jnp.sum(s, axis=-1, keepdims=True))).astype(BF)
                p_ref[i, 2 * pair + h] = p
                mixed.append(dot(p, w))
            o_ref[i, :, at : at + 128] = jnp.where(lo, mixed[0], mixed[1]).astype(BF)

    def project(x, layer, gain, qkv_ref):
        a = (norm_parts(x)[0] * gain).astype(BF)
        qkv_ref[...] = dot(a, r["wqkv"][layer]).astype(BF).reshape(ib, ROWS, 3 * D)

    x0 = r["x0"][pl.ds(step * ib, ib)].astype(F32).reshape(m, D)
    project(x0, 0, gains[0:1], r["qkv1"])
    for i in range(ib):
        attend_image(i, r["qkv1"], r["o1"], r["p1"])
    x1 = x0 + dot(r["o1"][...].reshape(m, D), r["wo"][0])
    r["x1"][...] = x1.reshape(ib, ROWS, D)
    b = (norm_parts(x1)[0] * gains[1:2]).astype(BF)
    x2 = x1
    for f in range(0, FF, 512):
        u, gp = gelu_parts(dot(b, r["win"][:, f : f + 512]))
        u = u.astype(BF)
        r["u"][:, :, f : f + 512] = u.reshape(ib, ROWS, 512)
        r["gp"][:, :, f : f + 512] = gp.astype(BF).reshape(ib, ROWS, 512)
        x2 = x2 + dot(u, r["wout"][f : f + 512])
    r["x2"][...] = x2.reshape(ib, ROWS, D)
    project(x2, 1, gains[2:3], r["qkv2"])

    def last(i, _):
        attend_image(i, r["qkv2"], r["o2"], r["p2"])
        x3 = r["x2"][i] + dot(r["o2"][i], r["wo"][1])
        r["x3"][i] = x3
        c = (norm_parts(x3)[0] * gains[3:4]).astype(BF)
        r["c"][i] = c
        if linked:
            r["c_scr"][step * ib + i] = c
            c_copy(step * ib + i).start()
        return 0

    lax.fori_loop(0, ib, last, 0)

    if linked:

        @pl.when(step == pl.num_programs(0) - 1)
        def _():
            for copy in early + [c_copy(i) for i in range(images)]:
                copy.wait()


def dense_forward(tokens, cot, routes, gains, wqkv, wo, win, wout, linked):
    n = tokens.shape[0] // PATCHES
    ib = 2 if n % 2 == 0 else 1

    def out(*shape, dtype=BF):
        return jax.ShapeDtypeStruct((n,) + shape, dtype)

    def block(shape):
        return pl.BlockSpec((ib,) + tuple(shape[1:]), lambda i: (i,) + (0,) * (len(shape) - 1))

    whole = pl.BlockSpec((n, ROWS, D), lambda i: (0, 0, 0))
    outs = [out(ROWS, D)] * 2 + [out(ROWS, D, dtype=F32)] * 3 + [out(ROWS, 3 * D)] * 2 + [out(ROWS, D)] * 2
    outs += [out(HEADS, ROWS, ROWS)] * 2 + [out(ROWS, FF)] * 2 + [out(ROWS, D)]
    out_specs = [whole, whole] + [block(o.shape) for o in outs[2:]]
    scratch = [pltpu.VMEM(((n - 1) * PATCHES + ROWS, D), F32)]
    params = dict(vmem_limit_bytes=62 << 20)
    if linked:
        outs += [out(ROWS, D)] * 2 + [jax.ShapeDtypeStruct(routes.shape, jnp.int32)]
        out_specs += [pl.BlockSpec(memory_space=pl.ANY)] * 3
        copies = pltpu.SemaphoreType.DMA((2 + n,))
        scratch += [pltpu.VMEM((n, ROWS, D), BF), copies, copies]
        params.update(collective_id=2, has_side_effects=True)
    return pl.pallas_call(
        functools.partial(fwd_kernel, linked),
        grid=(n // ib,),
        out_shape=outs,
        in_specs=[VMEM] * 8,
        out_specs=out_specs,
        scratch_shapes=scratch,
        compiler_params=pltpu.CompilerParams(**params),
        name="dense_forward",
    )(tokens, cot, routes, gains, wqkv, wo, win, wout)


def gate_rows(router_t, c, routes):
    logits = dot_t(router_t, c)
    expert = lax.broadcasted_iota(jnp.int32, logits.shape, 0)
    first, second = expert == routes[0:1], expert == routes[1:2]
    diff = jnp.sum(jnp.where(first, logits, 0.0) - jnp.where(second, logits, 0.0), axis=0, keepdims=True)
    return 1.0 / (1.0 + jnp.exp(-diff)), 1.0 / (1.0 + jnp.exp(diff)), first, second


def experts_kernel(groups, local, exp_axis, *refs):
    c_refs, g_refs, r_refs = refs[:groups], refs[groups : 2 * groups], refs[2 * groups : 3 * groups]
    router_t, win, wout = refs[3 * groups : 3 * groups + 3]
    outs = refs[3 * groups + 3 :]
    eg_ref, y_refs, d_refs, delta_refs = outs[0], outs[1 : groups + 1], outs[groups + 1 : 2 * groups + 1], outs[2 * groups + 1 : 3 * groups + 1]
    ci, cols, place, xg, slots, dy_scr, u_scr, gp_scr, stack, back, staged, count_v, count, plan, sem, load_sem, out_sem = outs[3 * groups + 1 :]
    n_tok = c_refs[0].shape[0]
    total = groups * n_tok
    images = total // ROWS
    step = pl.program_id(0)
    first_expert = lax.axis_index(exp_axis) * local

    def window(e, i):
        begin = plan[e * (images + 1) + i]
        return begin, pl.multiple_of(begin // 16 * 16, 16)

    def windows(i):
        most = jnp.int32(1)
        for e in range(local):
            at = window(e, i)[1]
            most = jnp.maximum(most, (plan[e * (images + 1) + i + 1] - at + 127) // 128)
        return most

    @pl.when(step == 0)
    def _():
        loads = []
        for k, (sources, first) in enumerate(((c_refs, 0), (g_refs, D + 128))):
            for s in range(groups):
                target = ci.at[pl.ds(s * n_tok, n_tok), pl.ds(first, D)]
                loads.append(pltpu.make_async_copy(sources[s], target, load_sem.at[k * groups + s]))
                loads[-1].start()
        for load in loads:
            load.wait()
        routes = jnp.concatenate([r[0:2] for r in r_refs], axis=1)
        g0, g1, _, _ = gate_rows(router_t[...], ci[:, 0:D], routes)
        expert_row = lax.broadcasted_iota(jnp.int32, (8, total), 0)
        mine, inside = first_expert + expert_row, expert_row < local
        is0, is1 = (mine == routes[0:1]) & inside, (mine == routes[1:2]) & inside
        member = jnp.where(is0 | is1, 1.0, 0.0)
        lane = lax.broadcasted_iota(jnp.int32, (8, total), 1)
        of_image = lax.broadcasted_iota(jnp.int32, (total, 128), 0) // ROWS
        of_image = jnp.where(of_image == lax.broadcasted_iota(jnp.int32, (total, 128), 1), 1.0, 0.0)
        count_v[...] = dot(member.astype(BF), of_image.astype(BF)).astype(jnp.int32)
        to_scalars = pltpu.make_async_copy(count_v, count, sem)
        to_scalars.start()
        upto = member
        shift = 1
        while shift < total:
            upto = upto + jnp.where(lane >= shift, pltpu.roll(upto, shift, 1), 0.0)
            shift *= 2
        to_scalars.wait()
        begin = jnp.int32(0)
        starts = []
        for e in range(local):
            starts.append(begin.astype(F32))
            plan[local * (images + 1) + 2 * e] = begin
            first = begin
            for i in range(images):
                plan[e * (images + 1) + i] = begin
                begin = begin + count[e, i]
            plan[e * (images + 1) + images] = begin
            plan[local * (images + 1) + 2 * e + 1] = begin - first
            begin = first + (begin - first + 127) // 128 * 128 + 256
        start = jnp.zeros((8, total), F32)
        for e in range(local):
            start = jnp.where(expert_row == e, starts[e], start)
        slot = start + jnp.where(member > 0, upto, 0.0)
        slot0 = jnp.sum(jnp.where(is0, slot, 0.0), axis=0, keepdims=True) - 1.0
        slot1 = jnp.sum(jnp.where(is1, slot, 0.0), axis=0, keepdims=True) - 1.0
        slot = jnp.where(member > 0, slot - 1.0, -1.0)
        for i in range(images):
            place[i] = slot[:, i * ROWS : (i + 1) * ROWS]
        gates = jnp.where(is0, g0, jnp.where(is1, g1, 0.0))
        sign = jnp.where(is0, 1.0, jnp.where(is1, -1.0, 0.0))
        slot_rows = jnp.where(expert_row == 0, slot0, jnp.where(expert_row == 1, slot1, 0.0))
        stacked = jnp.concatenate([gates, sign, slot_rows, jnp.zeros((104, total), F32)], axis=0)
        lane128 = lax.broadcasted_iota(jnp.int32, (128, 128), 1)
        for at in range(0, total, 128):
            col = stacked[:, at : at + 128].T
            cols[at : at + 128] = col
            low = col - col.astype(BF).astype(F32)
            info = jnp.where(lane128 < 16, col, jnp.where(lane128 < 24, pltpu.roll(low, 16, 1), 0.0))
            ci[at : at + 128, D : D + 128] = info.astype(BF)

        row = lax.broadcasted_iota(jnp.int32, (128, ROWS), 0)
        head = lax.broadcasted_iota(jnp.int32, (16, 2 * D + 128), 0)

        def gather(i, _):
            rows = ci[pl.ds(pl.multiple_of(i * ROWS, 16), ROWS)]

            def part(w, _):
                picks = []
                for e in range(local):
                    at = window(e, i)[1] + 128 * w
                    picks.append(jnp.where(place[i, e : e + 1] == (at + row).astype(F32), 1.0, 0.0).astype(BF))
                found = dot(jnp.concatenate(picks, axis=0), rows).astype(BF)
                for e in range(local):
                    begin, at = window(e, i)
                    at = pl.multiple_of(at + 128 * w, 16)
                    old = xg[pl.ds(at, 16)]
                    new = found[e * 128 : e * 128 + 16]
                    xg[pl.ds(at, 16)] = jnp.where(at + head < begin, old, new)
                    xg[pl.ds(pl.multiple_of(at + 16, 16), 112)] = found[e * 128 + 16 : e * 128 + 128]
                return 0

            return lax.fori_loop(0, windows(i), part, 0)

        lax.fori_loop(0, images, gather, 0)
        for e in range(local):
            end, at = window(e, images)
            xg[pl.ds(at, 16)] = jnp.where(at + head < end, xg[pl.ds(at, 16)], jnp.zeros(head.shape, BF))
            xg[pl.ds(pl.multiple_of(at + 16, 16), 240)] = jnp.zeros((240, 2 * D + 128), BF)

    begin, n = plan[local * (images + 1) + 2 * step], plan[local * (images + 1) + 2 * step + 1]

    def tile(row, size):
        at = pl.multiple_of(begin + row, 16)
        here = pl.ds(pl.multiple_of(row, 128), size)
        lane = lax.broadcasted_iota(jnp.int32, (size, 128), 1)
        x = xg[pl.ds(at, size), 0:D]
        info = xg[pl.ds(at, size), D : D + 128].astype(F32)
        g4r = xg[pl.ds(at, size), D + 128 :].astype(F32)
        gate = jnp.sum(jnp.where((lane == step) | (lane == step + 16), info, 0.0), axis=-1, keepdims=True)
        sign = jnp.sum(jnp.where(lane == step + 8, info, 0.0), axis=-1, keepdims=True)
        dy = (gate * g4r).astype(BF)
        dy_scr[here] = dy
        for f in range(0, FF, 512):
            u, gp = gelu_parts(dot(x, win[0, :, f : f + 512]))
            u_scr[here, f : f + 512] = u.astype(BF)
            gp_scr[here, f : f + 512] = gp.astype(BF)
        ey = dot(u_scr[here], wout[0]).astype(BF).astype(F32)
        dg = sign * jnp.sum(g4r * ey, axis=-1, keepdims=True)
        for f in range(0, FF, 512):
            du = dot_t(dy, wout[0, f : f + 512])
            gp_scr[here, f : f + 512] = (du * gp_scr[here, f : f + 512].astype(F32)).astype(BF)
        dcp = dot_t(gp_scr[here], win[0])
        slots[pl.ds(at, size), 0:D] = (gate * ey).astype(BF)
        slots[pl.ds(at, size), D : 2 * D] = dcp.astype(BF)
        low = dg - dg.astype(BF).astype(F32)
        slots[pl.ds(at, size), 2 * D :] = jnp.where(lane == 0, dg, jnp.where(lane == 1, low, 0.0)).astype(BF)

    whole = (n + TILE // 2 - 1) // TILE

    def full_tile(j, _):
        tile(j * TILE, TILE)
        return 0

    lax.fori_loop(0, whole, full_tile, 0)

    @pl.when(n > whole * TILE)
    def _():
        tile(whole * TILE, TILE // 2)
        rest = pl.ds(pl.multiple_of(whole * TILE + TILE // 2, 128), TILE // 2)
        for scratch in (dy_scr, u_scr, gp_scr):
            scratch[rest] = jnp.zeros((TILE // 2,) + scratch.shape[1:], BF)

    after = pl.multiple_of(begin + (n + 127) // 128 * 128, 16)
    slots[pl.ds(after, 256)] = jnp.zeros((256, 2 * D + 128), BF)

    rounded = (n + TILE - 1) // TILE

    @pl.when(rounded == 0)
    def _():
        eg_ref[...] = jnp.zeros_like(eg_ref)

    for tiles in range(1, u_scr.shape[0] // TILE + 1):

        @pl.when(rounded == tiles)
        def _(depth=tiles * TILE):
            x = xg[pl.ds(pl.multiple_of(begin, 16), depth), 0:D]
            dy = dy_scr[0:depth]
            for f in range(0, FF, D):
                eg_ref[0, 0, f : f + D] = t_dot(gp_scr[0:depth, f : f + D], x).astype(BF)
                eg_ref[0, 1, f : f + D] = t_dot(u_scr[0:depth, f : f + D], dy).astype(BF)

    @pl.when(step == local - 1)
    def _():
        lane = lax.broadcasted_iota(jnp.int32, (ROWS, 128), 1)

        def out_copies(s, i, slot):
            rows = pl.ds(pl.multiple_of(i * ROWS, 16), ROWS)
            return [
                pltpu.make_async_copy(staged.at[slot, k], target.at[rows], out_sem.at[slot, k])
                for k, target in enumerate((y_refs[s], d_refs[s]))
            ]

        def restore(s, i):
            image = s * (n_tok // ROWS) + i
            at_rows = pl.multiple_of(image * ROWS, 16)
            slot0, slot1 = cols[pl.ds(at_rows, ROWS), 16:17], cols[pl.ds(at_rows, ROWS), 17:18]

            def part(w):
                picks = []
                for e in range(local):
                    at = pl.multiple_of(window(e, image)[1] + 128 * w, 16)
                    stack[e * 128 : (e + 1) * 128] = slots[pl.ds(at, 128)]
                    slot = (at + lane).astype(F32)
                    picks.append(jnp.where((slot0 == slot) | (slot1 == slot), 1.0, 0.0).astype(BF))
                return dot(jnp.concatenate(picks, axis=1), stack[...])

            back[...] = part(0)

            def more(w, _):
                back[...] += part(w)
                return 0

            lax.fori_loop(1, windows(image), more, 0)
            slot = lax.rem(image, 2)

            @pl.when(image >= 2)
            def _():
                for copy in out_copies(s, i, slot):
                    copy.wait()

            staged[slot, 0] = back[:, 0:D].astype(BF)
            staged[slot, 1] = back[:, D : 2 * D].astype(BF)
            for copy in out_copies(s, i, slot):
                copy.start()
            cols[pl.ds(at_rows, ROWS)] = back[:, 2 * D :]

        for s in range(groups):

            def one(i, _, s=s):
                restore(s, i)
                return 0

            lax.fori_loop(0, n_tok // ROWS, one, 0)
        for slot in range(2):
            for copy in out_copies(groups - 1, 0, slot):
                copy.wait()
        for at in range(0, total, 128):
            place_t = cols[at : at + 128].T[0:8]
            s, left = divmod(at, n_tok)
            here = min(128, n_tok - left)
            delta_refs[s][:, left : left + here] = place_t[:, 0:here]
            if here < 128:
                delta_refs[s + 1][:, 0 : 128 - here] = place_t[:, here:]


def experts_all(cs, gs, rs, router_t, win, wout, slots_most, owners):
    groups = len(cs)
    local = win.shape[0]
    n_tok = cs[0].shape[0]
    total = groups * n_tok
    images = total // ROWS
    room = -(-(slots_most + local * 384 + TILE) // 128) * 128
    width = 2 * D + 128
    deepest = -(-slots_most // local // TILE) * TILE

    def full(shape):
        return pl.BlockSpec(tuple(shape), lambda i: (0,) * len(shape))

    outs = [jax.ShapeDtypeStruct((local, 2, FF, D), BF)]
    outs += [jax.ShapeDtypeStruct((n_tok, D), BF)] * (2 * groups)
    outs += [jax.ShapeDtypeStruct((8, n_tok), F32)] * groups
    vm = pltpu.VMEM
    result = pl.pallas_call(
        functools.partial(experts_kernel, groups, local, "exp"),
        grid=(local,),
        out_shape=outs,
        in_specs=[pl.BlockSpec(memory_space=pl.ANY)] * (2 * groups)
        + [VMEM] * (groups + 1)
        + [pl.BlockSpec((1, D, FF), lambda i: (i, 0, 0)), pl.BlockSpec((1, FF, D), lambda i: (i, 0, 0))],
        out_specs=[pl.BlockSpec((1, 2, FF, D), lambda i: (i, 0, 0, 0))]
        + [pl.BlockSpec(memory_space=pl.ANY)] * (2 * groups)
        + [full(o.shape) for o in outs[2 * groups + 1 :]],
        scratch_shapes=[
            vm((total, width), BF),
            vm((total, 128), F32),
            vm((images, 8, ROWS), F32),
            vm((room, width), BF),
            vm((room, width), BF),
            vm((deepest, D), BF),
            vm((deepest, FF), BF),
            vm((deepest, FF), BF),
            vm((local * 128, width), BF),
            vm((ROWS, width), F32),
            vm((2, 2, ROWS, D), BF),
            vm((8, 128), jnp.int32),
            pltpu.SMEM((8, 128), jnp.int32),
            pltpu.SMEM((local * (images + 3),), jnp.int32),
            pltpu.SemaphoreType.DMA(()),
            pltpu.SemaphoreType.DMA((2 * groups,)),
            pltpu.SemaphoreType.DMA((2, 2)),
        ],
        compiler_params=pltpu.CompilerParams(vmem_limit_bytes=62 << 20),
        name="experts",
    )(*cs, *gs, *rs, router_t, win, wout)
    eg = result[0].reshape((local, 2) + owners + (FF // math.prod(owners), D))
    return eg, result[1 : groups + 1], result[groups + 1 : 2 * groups + 1], result[2 * groups + 1 :]


class Halving:
    def __init__(self, place, links, total, dims, order, received, lead=()):
        self.p, self.links, self.total, self.dims, self.order = place, links, total, dims, order
        self.received, self.lead = received, lead
        self.first = links.reserve(len(order) + 2 * order.count("z"))

    def where(self, fixed):
        return (slice(None),) * len(self.lead) + tuple(fixed.get(b, slice(None)) for b in self.dims)

    def copies(self, k):
        b = self.order[k]
        fixed = {q: self.p.bit[q] for q in self.order[:k]}
        if b == "z":
            return [
                self.links.copy(self.first + k + n, self.total.at[self.where({**fixed, **bits})], self.received[k].at[n], device)
                for n, (bits, device) in enumerate(self.p.others)
            ]
        fixed[b] = 1 - self.p.bit[b]
        return [self.links.copy(self.first + k, self.total.at[self.where(fixed)], self.received[k], self.p.partner[b])]

    def add(self, fixed, other, other_dims):
        free = [b for b in self.dims if b not in fixed]
        sizes = list(self.lead) + [2] * len(free)

        def block(i, _):
            at = []
            for size in reversed(sizes):
                at.insert(0, i % size)
                i = i // size
            full = dict(fixed, **dict(zip(free, at[len(self.lead) :])))
            mine = self.total.at[tuple(at[: len(self.lead)]) + tuple(full[b] for b in self.dims)]
            term = other.at[tuple(at[: len(self.lead)]) + tuple(full[b] for b in other_dims)]
            mine[...] = (mine[...].astype(F32) + term[...].astype(F32)).astype(BF)
            return 0

        lax.fori_loop(0, math.prod(sizes), block, 0)

    def step(self, k, other=None):
        fixed = {q: self.p.bit[q] for q in self.order[:k] if q != "z"}
        other_dims = [b for b in self.dims if b not in fixed]
        if k:
            for copy in self.copies(k - 1):
                copy.wait()
            other = self.received[k - 1]
        if k == len(self.order) and self.order[-1] == "z":
            mine = self.own()
            total = mine[...].astype(F32)
            for n in range(len(self.p.others)):
                total = total + other[n].astype(F32)
            mine[...] = total.astype(BF)
        elif k < len(self.order) and self.order[k] != "z":
            b = self.order[k]
            self.add(dict(fixed, **{b: 1 - self.p.bit[b]}), other, other_dims)
            self.copies(k)[0].start()
            self.add(dict(fixed, **{b: self.p.bit[b]}), other, other_dims)
        else:
            self.add(fixed, other, other_dims)
            if k < len(self.order):
                for copy in self.copies(k):
                    copy.start()

    def own(self):
        return self.total.at[self.where(self.p.bit)]


class ExpertSum:
    def __init__(self, place, links, j, slot, eg, own, part, received, order, out, local_sem):
        self.p, self.links, self.out = place, links, out.at[j]
        self.given = eg.at[j]
        self.mine = own.at[slot]
        self.load = pltpu.make_async_copy(self.given.at[:, :, :, :, place.bit["c"]], self.mine, local_sem.at[slot])
        self.core = links.copy(
            links.reserve(1), self.given.at[:, :, :, :, 1 - place.bit["c"]], part.at[j], place.partner["c"]
        )
        self.halving = Halving(place, links, part.at[j], "hlx", order, received, lead=(2,))

    def run(self, k):
        if k == 0:
            self.core.start()
            return
        if k == 1:
            self.load.wait()
            self.core.wait()
        self.halving.step(k - 1, self.mine)
        if k == 4:
            self.out[...] = self.halving.own()[...].astype(F32)


class SharedSum:
    def __init__(self, place, links, src, core_rx, received, order, out):
        self.p, self.links, self.order, self.out, self.core_rx = place, links, order, out, core_rx
        self.core = links.copy(links.reserve(1), src.at[1 - place.bit["c"]], core_rx, place.partner["c"])
        self.halving = Halving(place, links, src.at[place.bit["c"]], "yxhl", order, received)
        self.first = links.reserve(len(order) + 3)

    def back(self, k):
        known = "c" + self.order[: len(self.order) - k] if k <= len(self.order) else ""
        bits = known.replace("z", "hl")
        mine = self.out.at[tuple(self.p.bit[b] if b in bits else slice(None) for b in BITS)]
        if known[-1] == "z":
            return [self.links.copy(self.first + n, mine, mine, device) for n, (_, device) in enumerate(self.p.others)]
        return [self.links.copy(self.first + 2 + k, mine, mine, self.p.partner[known[-1]])]

    def run(self, k):
        n = len(self.order)
        if k == 0:
            self.core.start()
        elif k <= n:
            if k == 1:
                self.core.wait()
            self.halving.step(k - 1, self.core_rx)
        elif k == n + 1:
            self.halving.step(n)
            self.out[tuple(self.p.bit[b] for b in BITS)] = self.halving.own()[...]
            for copy in self.back(0):
                copy.start()
        else:
            for copy in self.back(k - n - 2):
                copy.wait()
            if k <= 2 * n + 1:
                for copy in self.back(k - n - 1):
                    copy.start()


class SmallSum:
    def __init__(self, place, links, src, rx):
        self.p, self.links, self.src, self.rx = place, links, src, rx
        self.first = links.reserve(len(BITS))

    def copy(self, k):
        return self.links.copy(self.first + k, self.src.at[k], self.rx.at[k], self.p.partner[BITS[k]])

    def run(self, k, out):
        if k:
            self.copy(k - 1).wait()
            total = self.src[k - 1] + self.rx[k - 1]
            if k == len(BITS):
                out[...] = total
                return
            self.src[k] = total
        self.copy(k).start()


GROUPS = ((48, "yxz"), (48, "xyz"), (48, "yxz"), (32, "yxz"), (16, "xyz"))
GROUP_ROWS = (0, 1536, 3072, 4608, 5632)
EXPERT_ORDERS = ("lhx", "xlh", "xlh", "xlh")

ORDER = (
    ("E", 0, 0), ("d", 0, 0), ("d", 1, 0), ("E", 1, 0), ("run", 0, 0), ("E", 1, 1), ("d", 2, 0), ("E", 2, 0),
    ("d", 3, 0), ("E", 0, 1), ("run", 1, 0), ("y", 0, 0), ("E", 3, 0), ("run", 2, 0), ("E", 2, 1), ("run", 3, 0),
    ("run", 4, 0), ("run", 5, 0), ("E", 1, 2), ("run", 6, 0), ("run", 7, 0), ("S", 0, 0), ("E", 0, 2), ("run", 8, 0),
    ("E", 3, 1), ("run", 9, 0), ("run", 10, 0), ("run", 11, 0), ("run", 12, 0), ("S", 0, 1), ("S", 2, 0), ("E", 2, 2),
    ("run", 13, 0), ("S", 1, 0), ("run", 14, 0), ("S", 1, 1), ("S", 2, 1), ("E", 1, 3), ("run", 15, 0), ("S", 0, 2),
    ("run", 16, 0), ("E", 3, 2), ("run", 17, 0), ("S", 2, 2), ("run", 18, 0), ("S", 3, 0), ("S", 0, 3), ("S", 1, 2),
    ("E", 1, 4), ("run", 19, 0), ("S", 2, 3), ("S", 4, 0), ("S", 3, 1), ("S", 0, 4), ("S", 4, 1), ("S", 1, 3),
    ("S", 2, 4), ("S", 3, 2), ("S", 4, 2), ("S", 0, 5), ("S", 4, 3), ("few", 0, 0), ("S", 3, 3), ("S", 1, 4),
    ("few", 1, 0), ("S", 0, 6), ("few", 2, 0), ("S", 2, 5), ("S", 4, 4), ("S", 3, 4), ("E", 0, 3), ("few", 3, 0),
    ("S", 1, 5), ("S", 4, 5), ("S", 3, 5), ("S", 2, 6), ("E", 3, 3), ("run", 20, 0), ("S", 0, 7), ("S", 1, 6),
    ("few", 4, 0), ("S", 3, 6), ("S", 4, 6), ("E", 2, 3), ("E", 3, 4), ("E", 0, 4), ("S", 1, 7), ("few", 5, 0),
    ("S", 2, 7), ("S", 4, 7), ("S", 3, 7), ("S", 0, 8), ("S", 2, 8), ("S", 1, 8), ("S", 4, 8), ("E", 2, 4),
    ("S", 3, 8),
)

LOADED = ("c", "x3", "cot", "d", "delta", "x2", "qkv", "o", "p", "wo", "wqkv", "x1", "wout", "gp", "u", "win", "y", "x0")


def bwd_kernel(linked, *refs):
    names = ["gains", "router_t", "routes", "wqkv", "wo", "win", "wout", "x0", "x1", "x2", "x3", "qkv1", "qkv2"]
    names += ["o1", "o2", "p1", "p2", "u", "gp", "c", "cot", "d", "delta", "y"]
    if linked:
        names += ["d_send", "delta_send", "y_send", "eg"]
    names += ["act_out", "gin_out", "small_out"]
    if linked:
        names += ["eg_out"] + ["out" + str(g) for g in range(len(GROUPS))]
    else:
        names += ["shared_out"]
    names += ["v_" + n for n in LOADED] + ["gv", "a_scr", "dbr_scr", "dqkv_scr", "sem"]
    if linked:
        names += ["d_rx", "delta_rx", "y_rx", "own", "part", "small_src", "small_rx", "eg_sem", "send", "recv"]
        names += ["src" + str(g) for g in range(len(GROUPS))]
        names += ["rx" + str(g) + str(k) for g, (_, order) in enumerate(GROUPS) for k in range(len(order) + 1)]
        names += ["erx" + str(j) + str(k) for j in range(len(EXPERT_ORDERS)) for k in range(3)]
    r = dict(zip(names, refs, strict=True))
    gains, gv, a_scr, dbr_scr, dqkv_scr = (r[n] for n in ("gains", "gv", "a_scr", "dbr_scr", "dqkv_scr"))
    images = gv.shape[0]
    m = images * ROWS
    lo = lane_low(ROWS)

    second = {"qkv": "qkv2", "o": "o2", "p": "p2"}
    copies = {}

    def fetch(name, source):
        copies[name] = pltpu.make_async_copy(r[source], r["v_" + name], r["sem"].at[LOADED.index(name)])
        copies[name].start()

    def need(*wanted):
        for name in wanted:
            copies[name].wait()

    if linked:
        place = Place()
        links = Links(r["send"], r["recv"])
        place.meet([place.partner[b] for b in "cyx"] + [device for _, device in place.others])
        beside = place.partner["y"]
        delta_copy = links.copy(links.reserve(1), r["delta_send"], r["delta_rx"], beside)
        delta_copy.start()
        d_first = links.reserve(images)

        def d_copy(i):
            return links.copy(d_first + i, r["d_send"].at[i], r["d_rx"].at[i], beside)

        turn = [at for kind, at, what in ORDER if (kind, what) == ("E", 1)]
        experts = [
            ExpertSum(
                place, links, j, turn.index(j) % 2, r["eg"], r["own"], r["part"], [r["erx" + str(j) + str(k)] for k in range(3)],
                order, r["eg_out"], r["eg_sem"],
            )
            for j, order in enumerate(EXPERT_ORDERS)
        ]
        experts[turn[0]].load.start()
        experts[turn[1]].load.start()
        y_copy = links.copy(links.reserve(1), r["y_send"], r["y_rx"], beside)
        sums = []
        for g, (_, order) in enumerate(GROUPS):
            rx = [r["rx" + str(g) + str(k)] for k in range(len(order) + 1)]
            sums.append(SharedSum(place, links, r["src" + str(g)], rx[0], rx[1:], order, r["out" + str(g)]))
        few = SmallSum(place, links, r["small_src"], r["small_rx"])
        small = r["small_src"].at[0]
        small[...] = jnp.zeros(small.shape, F32)
    else:
        small = r["small_out"]
    for name in LOADED:
        fetch(name, second.get(name, name))

    def keep(block, value):
        value = value.astype(BF)
        if not linked:
            r["shared_out"][block] = value
            return
        row, end = block * D, block * D + D
        for g, (share, _) in enumerate(GROUPS):
            base, cell = GROUP_ROWS[g], 4 * share
            for q in range(8):
                at = base + q * cell
                if row <= at and at + cell <= end:
                    part = value[at - row : at - row + cell]
                    r["src" + str(g)][q // 4, q // 2 % 2, q % 2] = part.reshape(2, 2, share, D)

    def router():
        need("c", "delta")
        c_all = r["v_c"][...].reshape(m, D)
        g0, g1, first, other = gate_rows(r["router_t"][...], c_all, r["routes"][...])
        delta = r["v_delta"][0:1] + r["v_delta"][1:2]
        if linked:
            delta_copy.wait()
            delta = delta + (r["delta_rx"][0:1] + r["delta_rx"][1:2])
        dl = g0 * g1 * delta
        dlog = jnp.where(first, dl, jnp.where(other, -dl, 0.0)).astype(BF)
        small[4 : 4 + dlog.shape[0]] = dot(dlog, c_all)
        small[0:4] = jnp.zeros((4, D), F32)
        gv[...] = t_dot(dlog, r["router_t"][...]).reshape(images, ROWS, D)
        need("x3", "cot", "d")

    def add_gain(row, by_gain):
        small[row : row + 1] += jnp.sum(by_gain, axis=0, keepdims=True)

    def first(i):
        dc = gv[i] + r["v_d"][i].astype(F32)
        if linked:
            d_copy(i).wait()
            dc = dc + r["d_rx"][i].astype(F32)
        dx, by_gain = norm_back(dc, r["v_x3"][i], gains[3:4])
        gv[i] = r["v_cot"][i].astype(F32) + dx
        add_gain(3, by_gain)
        if i == 0:
            need("x2", "qkv", "o", "p", "wo")
        attend_image(i, 1, gains[2:3], r["v_x2"])

    def attend_image(i, layer, gain, x):
        qkv, o, p = r["v_qkv"], r["v_o"], r["v_p"]
        a_scr[i] = (norm_parts(x[i].astype(F32))[0] * gain).astype(BF)
        dbr = gv[i].astype(BF)
        dbr_scr[i] = dbr
        do = dot_t(dbr, r["v_wo"][layer]).astype(BF)
        dod = do.astype(F32) * o[i].astype(F32)
        for pair in range(HEADS // 2):
            at = 128 * pair
            q = qkv[i, :, at : at + 128] * BF(0.125)
            k = qkv[i, :, D + at : D + at + 128]
            w = qkv[i, :, 2 * D + at : 2 * D + at + 128]
            dqs, dk, dw = [], 0.0, 0.0
            for h in range(2):
                mask = lo if h == 0 else ~lo
                dom = jnp.where(mask, do[:, at : at + 128], BF(0))
                inner = jnp.sum(jnp.where(mask, dod[:, at : at + 128], 0.0), axis=-1, keepdims=True)
                ph = p[i, 2 * pair + h]
                ds = (ph.astype(F32) * (dot_t(dom, w) - inner)).astype(BF)
                dw = dw + t_dot(ph, dom)
                dqs.append(dot(ds, k))
                dk = dk + t_dot(ds, jnp.where(mask, q, BF(0)))
            dqkv_scr[i, :, at : at + 128] = (jnp.where(lo, dqs[0], dqs[1]) * 0.125).astype(BF)
            dqkv_scr[i, :, D + at : D + at + 128] = dk.astype(BF)
            dqkv_scr[i, :, 2 * D + at : 2 * D + at + 128] = dw.astype(BF)

    def attend_weights(block):
        a_all = a_scr[...].reshape(m, D)
        for f in range(3):
            keep(block + f, t_dot(a_all, dqkv_scr[:, :, f * D : f * D + D].reshape(m, D)))
        keep(block + 3, t_dot(r["v_o"][...].reshape(m, D), dbr_scr[...].reshape(m, D)))

    def close(x, layer, row, out):
        def image(i, _):
            da = dot_t(dqkv_scr[i], r["v_wqkv"][layer])
            dx, by_gain = norm_back(da, x[i].astype(F32), gains[row : row + 1])
            out[i] = gv[i] + dx
            add_gain(row, by_gain)
            return 0

        lax.fori_loop(0, images, image, 0)

    def first_close():
        for name in ("qkv", "o", "p"):
            fetch(name, name + "1")
        need("wqkv")
        close(r["v_x2"], 1, 2, gv)
        need("x1", "wout", "gp", "u", "win")

    gp = r["v_gp"]

    def mlp(i):
        a_scr[i] = (norm_parts(r["v_x1"][i])[0] * gains[1:2]).astype(BF)
        dm = gv[i].astype(BF)
        dbr_scr[i] = dm
        for f in range(0, FF, 512):
            du = dot_t(dm, r["v_wout"][f : f + 512])
            gp[i, :, f : f + 512] = (du * gp[i, :, f : f + 512].astype(F32)).astype(BF)

    def mlp_out_weights():
        dm_all = dbr_scr[...].reshape(m, D)
        for f in range(4):
            keep(4 + f, t_dot(r["v_u"][:, :, f * D : f * D + D].reshape(m, D), dm_all))

    def mlp_in_weights():
        b_all = a_scr[...].reshape(m, D)
        for f in range(4):
            keep(8 + f, t_dot(b_all, gp[:, :, f * D : f * D + D].reshape(m, D)))

    def mlp_close():
        def image(i, _):
            db = dot_t(gp[i], r["v_win"][...])
            dx, by_gain = norm_back(db, r["v_x1"][i], gains[1:2])
            gv[i] = gv[i] + dx
            add_gain(1, by_gain)
            return 0

        lax.fori_loop(0, images, image, 0)
        need("x0", "qkv", "o", "p")

    def last(i):
        attend_image(i, 0, gains[0:1], r["v_x0"])

    def last_close():
        close(r["v_x0"], 0, 0, r["gin_out"])

    def act():
        need("y")
        if linked:
            y_copy.wait()
        for i in range(images):
            x4 = r["v_x3"][i] + r["v_y"][i].astype(F32)
            if linked:
                x4 = x4 + r["y_rx"][i].astype(F32)
            r["act_out"][i] = x4.astype(BF)

    compute = [router] + [functools.partial(first, i) for i in range(images)]
    compute += [lambda: attend_weights(0), first_close] + [functools.partial(mlp, i) for i in range(images)]
    compute += [mlp_out_weights, mlp_in_weights, mlp_close] + [functools.partial(last, i) for i in range(images)]
    compute += [lambda: attend_weights(12), last_close, act]
    if not linked:
        for step in compute:
            step()
        return
    done = 0
    for kind, at, what in ORDER:
        if kind == "run":
            compute[done]()
            done += 1
        elif kind == "d":
            d_copy(at).start()
        elif kind == "y":
            y_copy.start()
        elif kind == "few":
            few.run(at, r["small_out"])
        elif kind == "E":
            experts[at].run(what)
            if what == 1 and turn.index(at) + 2 < len(turn):
                experts[turn[turn.index(at) + 2]].load.start()
        else:
            sums[at].run(what)


def dense_backward(weights, router_t, routes, saved, cot, d, delta, y, sent=None):
    gains, wqkv, wo, win, wout = weights
    x0, x1, x2, x3, qkv1, qkv2, o1, o2, p1, p2, u, gp, c = saved
    images = x0.shape[0]
    linked = sent is not None
    small_rows = 16 if linked else 4 + router_t.shape[0]
    ins = [gains, router_t, routes, wqkv, wo, win, wout, *saved, cot, d, delta, y] + (list(sent) if linked else [])
    outs = [
        jax.ShapeDtypeStruct((images, ROWS, D), BF),
        jax.ShapeDtypeStruct((images, ROWS, D), F32),
        jax.ShapeDtypeStruct((small_rows, D), F32),
    ]
    if not linked:
        outs.append(jax.ShapeDtypeStruct((16, D, D), BF))
    vm = pltpu.VMEM
    loaded = dict(
        c=c, x3=x3, cot=cot, d=d, delta=delta, x2=x2, qkv=qkv1, o=o1, p=p1, wo=wo, wqkv=wqkv, x1=x1, wout=wout,
        gp=gp, u=u, win=win, y=y, x0=x0,
    )
    scratch = [vm(loaded[name].shape, loaded[name].dtype) for name in LOADED]
    scratch += [vm((images, ROWS, D), F32), vm((images, ROWS, D), BF), vm((images, ROWS, D), BF)]
    scratch += [vm((images, ROWS, 3 * D), BF), pltpu.SemaphoreType.DMA((len(LOADED),))]
    params = dict(vmem_limit_bytes=62 << 20)
    if linked:
        eg = sent[-1]
        local, share = eg.shape[0], eg.shape[-2]
        outs.append(jax.ShapeDtypeStruct((local, 2, share, D), F32))
        outs += [jax.ShapeDtypeStruct((2,) * 5 + (rows, D), BF) for rows, _ in GROUPS]
        copies = 2 + images + 4 * local + 15 * len(GROUPS) + len(BITS)
        scratch += [vm(d.shape, BF), vm(delta.shape, F32), vm(y.shape, BF)]
        scratch += [
            vm((2, 2, 2, 2, 2, share, D), BF),
            vm((local, 2, 2, 2, 2, share, D), BF),
            vm((len(BITS), small_rows, D), F32),
            vm((len(BITS), small_rows, D), F32),
            pltpu.SemaphoreType.DMA((2,)),
            pltpu.SemaphoreType.DMA((copies,)),
            pltpu.SemaphoreType.DMA((copies,)),
        ]
        scratch += [vm((2,) * 5 + (rows, D), BF) for rows, _ in GROUPS]
        for rows, order in GROUPS:
            scratch += [vm((2,) * (4 - k) + (rows, D), BF) for k in range(len(order.strip("z")) + 1)]
            if "z" in order:
                scratch.append(vm((3, rows, D), BF))
        scratch += [vm((2,) * (3 - k) + (share, D), BF) for _ in EXPERT_ORDERS for k in range(3)]
        params.update(collective_id=1, has_side_effects=True)
    return pl.pallas_call(
        functools.partial(bwd_kernel, linked),
        out_shape=outs,
        in_specs=[VMEM] * 3 + [pl.BlockSpec(memory_space=pl.ANY)] * (len(ins) - 3),
        out_specs=[VMEM] * len(outs),
        scratch_shapes=scratch,
        compiler_params=pltpu.CompilerParams(**params),
        name="dense_backward",
    )(*ins)


def finish_kernel(n_shared, act, gin, small, eg, *refs):
    shared, refs = refs[:n_shared], refs[n_shared:]
    act_out, gin_out, qkv_out, proj_out, gain_out, mlp_in_out, mlp_out_out, router_out, in_out, out_out = refs[:10]
    v_shared, v_wide, v_gin, v_act, in_sem, out_sem = refs[10:]
    images = act.shape[0]
    blocks = v_wide.shape[0]
    targets = {3: proj_out.at[1], 15: proj_out.at[0]}
    for f in range(3):
        targets[f] = qkv_out.at[1, :, pl.ds(f * D, D)]
        targets[12 + f] = qkv_out.at[0, :, pl.ds(f * D, D)]
    for f in range(4):
        targets[4 + f] = mlp_out_out.at[pl.ds(f * D, D)]
        targets[8 + f] = mlp_in_out.at[:, pl.ds(f * D, D)]
    loads, at = [], 0
    for k, part in enumerate(shared):
        rows = part.shape[0]
        loads.append((at, pltpu.make_async_copy(part, v_shared.at[pl.ds(at, rows)], in_sem.at[k])))
        at += rows
    load_gin = pltpu.make_async_copy(gin, v_gin, in_sem.at[n_shared])
    load_act = pltpu.make_async_copy(act, v_act, in_sem.at[n_shared + 1])
    for _, load in loads:
        load.start()
    load_gin.start()
    load_act.start()

    def store(b):
        return pltpu.make_async_copy(v_wide.at[b], targets[b], out_sem.at[b])

    waited = 0
    for b in range(blocks):
        while waited < n_shared and loads[waited][0] < (b + 1) * D:
            loads[waited][1].wait()
            waited += 1
        v_wide[b] = v_shared[b * D : (b + 1) * D].astype(F32)
        store(b).start()
    gain_out[...] = small[0:4]
    router_out[...] = small[4 : 4 + router_out.shape[0]]
    for e in range(eg.shape[0]):
        in_out[e] = eg[e, 0]
        out_out[e] = eg[e, 1]
    load_gin.wait()
    load_act.wait()
    for i in range(images):
        gin_out[i * PATCHES : (i + 1) * PATCHES] = v_act[i, 0:PATCHES].astype(F32)
    act_out[...] = gin_out[...].astype(BF)
    for i in range(images):
        gin_out[i * PATCHES : (i + 1) * PATCHES] = v_gin[i, 0:PATCHES]
    for b in range(blocks):
        store(b).wait()


def finish(act, gin, shared, small, eg, experts):
    images, local, share = act.shape[0], eg.shape[0], eg.shape[2]
    row_count = images * PATCHES
    blocks = 16
    outs = [
        jax.ShapeDtypeStruct((row_count, D), BF),
        jax.ShapeDtypeStruct((row_count, D), F32),
        jax.ShapeDtypeStruct((2, D, 3 * D), F32),
        jax.ShapeDtypeStruct((2, D, D), F32),
        jax.ShapeDtypeStruct((4, D), F32),
        jax.ShapeDtypeStruct((D, FF), F32),
        jax.ShapeDtypeStruct((FF, D), F32),
        jax.ShapeDtypeStruct((experts, D), F32),
        jax.ShapeDtypeStruct((local, share, D), F32),
        jax.ShapeDtypeStruct((local, share, D), F32),
    ]
    far = pl.BlockSpec(memory_space=pl.ANY)
    return pl.pallas_call(
        functools.partial(finish_kernel, len(shared)),
        out_shape=outs,
        in_specs=[far, far, VMEM, VMEM] + [far] * len(shared),
        out_specs=[VMEM, VMEM, far, far, VMEM, far, far, VMEM, VMEM, VMEM],
        scratch_shapes=[
            pltpu.VMEM((blocks * D, D), BF),
            pltpu.VMEM((blocks, D, D), F32),
            pltpu.VMEM(gin.shape, F32),
            pltpu.VMEM(act.shape, BF),
            pltpu.SemaphoreType.DMA((len(shared) + 2,)),
            pltpu.SemaphoreType.DMA((blocks,)),
        ],
        compiler_params=pltpu.CompilerParams(vmem_limit_bytes=62 << 20),
        name="finish",
    )(act, gin, small, eg, *shared)


def from_peer(array, groups, shift):
    return lax.ppermute(array, "exp", [(i, (i + shift) % groups) for i in range(groups)])


def shards(
    tokens, routes, norm_gains, attn_qkv, attn_out, mlp_in, mlp_out, router, experts_in, experts_out, cotangent
):
    row_count = tokens.shape[0]
    groups = lax.axis_size("exp")
    local = experts_in.shape[0]
    choices = routes.shape[1]
    capacity = 2 * choices * row_count // (local * groups)
    images = row_count // PATCHES
    n_tok = images * ROWS
    routes_t = routes.T.reshape(choices, images, PATCHES)
    routes_t = jnp.pad(routes_t, ((0, 8 - choices), (0, 0), (0, ROWS - PATCHES)), constant_values=-1)
    routes_t = routes_t.reshape(8, n_tok)
    router_t = router.T
    rep = lax.axis_size("rep")
    known = (rep, groups, local) == (16, 2, 4)
    owners = (2, 2, 2, 2) if known else (rep,)
    x0, cot, x1, x2, x3, qkv1, qkv2, o1, o2, p1, p2, u, gp, c, *received = dense_forward(
        tokens, cotangent, routes_t, norm_gains, attn_qkv, attn_out, mlp_in, mlp_out, known
    )

    def of_all(mine, place):
        if known:
            others = [received[place]]
        else:
            others = [from_peer(mine, groups, k) for k in range(1, groups)]
        return [part.reshape(-1, part.shape[-1]) for part in [mine] + others]

    cs, gs, rs = of_all(c, 0), of_all(cot, 1), of_all(routes_t, 2)
    eg, ys, ds, deltas = experts_all(
        cs, gs, rs, router_t, experts_in, experts_out, local * capacity * groups, owners
    )

    weights = (norm_gains, attn_qkv, attn_out, mlp_in, mlp_out)
    saved = (x0, x1, x2, x3, qkv1, qkv2, o1, o2, p1, p2, u, gp, c)
    by_image = (images, ROWS, D)
    experts = router_t.shape[0]
    if known:
        sent = (ds[1].reshape(by_image), deltas[1], ys[1].reshape(by_image), eg)
        act, gin, small, eg, *shared = dense_backward(
            weights, router_t, routes_t, saved, cot, ds[0].reshape(by_image), deltas[0], ys[0].reshape(by_image), sent
        )
        shared = [part.reshape(-1, D) for part in shared]
    else:

        def back(parts):
            total = parts[0].astype(F32)
            for k in range(1, groups):
                total = total + from_peer(parts[k], groups, groups - k).astype(F32)
            return total

        d, delta, y = back(ds).astype(BF), back(deltas), back(ys).astype(BF)
        act, gin, small, shared = dense_backward(
            weights, router_t, routes_t, saved, cot, d.reshape(by_image), delta, y.reshape(by_image)
        )
        eg = lax.psum_scatter(eg, "rep", scatter_dimension=2, tiled=True).reshape(local, 2, FF // rep, D).astype(F32)
        shared, small = lax.psum((shared, small), ("rep", "exp"))
        shared = [shared.reshape(-1, D)]
    outs = list(finish(act, gin, shared, small, eg, experts))
    outs[7] = outs[7].T
    outs[8] = jnp.swapaxes(outs[8], 1, 2)
    return tuple(outs)


def solution(mesh):
    rows = P(("rep", "exp"), None)
    return jax.shard_map(
        shards,
        mesh=mesh,
        in_specs=(rows, rows, P(), P(), P(), P(), P(), P(), P("exp", None, None), P("exp", None, None), rows),
        out_specs=(rows, rows, P(), P(), P(), P(), P(), P(), P("exp", None, "rep"), P("exp", "rep", None)),
        check_vma=False,
    )
```

profile of v0, /device:TPU:0, one launch (start us, length us, event | category | flops | bytes accessed | tf_op | source)
XLA Modules:
  0.0 204.2 jit_solution(3566632236903611)
XLA Ops:
  0.6 0.8 reshape.68
  1.4 0.7 reshape.69.refs_2_.refs_4_
  2.1 39.1 %dense_forward.1 = (bf16[4,208,384]{2,1,0:T(8,128)(2,1)}, bf16[4,208,384]{2,1,0:T(8,128)(2,1)}, f32[4,208,384]{2,1,0:T(8,128)}, f32[4,208,384]{2,1,0:T(8,128)}, ...) custom-call(bf16[788,384]{1,0:T(8,128)(2,1)} %refs_0_.2, ...), custom_call_target="tpu_custom_call" | custom-call | tf_op jit(solution)/shard_map/dense_forward/pallas_call | solution.py:225
  41.3 42.6 %experts.1 = (bf16[4,2,1536,384]{3,2,1,0:T(8,128)(2,1)}, bf16[832,384]{1,0:T(8,128)(2,1)}, bf16[832,384]{1,0:T(8,128)(2,1)}, bf16[832,384]{1,0:T(8,128)(2,1)}, b...) custom-call(bf16[832,384]{1,0:T(8,128)(2,1)} %bitcast.20, bf16[832,384]{1,0:T(8,128)(2,1)} %bitcast.29, ...), custom_call_target="tpu_custom_call" | custom-call | tf_op jit(solution)/shard_map/experts/pallas_call | solution.py:501
  83.9 111.9 %dense_backward.1 = (bf16[4,208,384]{2,1,0:T(8,128)(2,1)}, f32[4,208,384]{2,1,0:T(8,128)}, f32[16,384]{1,0:T(8,128)}, f32[4,2,96,384]{3,2,1,0:T(8,128)}, bf16[2,...) custom-call(f32[4,384]{1,0:T(4,128)} %refs_0_.3, ...), custom_call_target="tpu_custom_call" | custom-call | tf_op jit(solution)/shard_map/dense_backward/pallas_call | solution.py:984
  195.8 8.2 %finish.1 = (bf16[788,384]{1,0:T(8,128)(2,1)}, f32[788,384]{1,0:T(8,128)}, f32[2,384,1152]{2,1,0:T(8,128)}, f32[2,384,384]{2,1,0:T(8,128)}, f32[4,384]{1,0:T(4,1...) custom-call(bf16[4,208,384]{2,1,0:T(8,128)(2,1)} %get-tuple-element., ...), custom_call_target="tpu_custom_call" | custom-call | tf_op jit(solution)/shard_map/finish/pallas_call | solution.py:1063
  (1 shorter events, 0.0 us)
where the time goes:
time: 208 us; the launch traced here: 204 us
  Pallas kernels  202 us (97%)
    pallas_call x1, Pallas kernels, dense_backward(): pl.pallas_call(functools.partial(bwd_kernel, linked), out_shape=outs, in_...  112 us
    pallas_call x1, Pallas kernels, experts_all(): pl.pallas_call(functools.partial(experts_kernel, groups, local, 'exp'), g...  42.6 us
    pallas_call x1, Pallas kernels, dense_forward(): pl.pallas_call(functools.partial(fwd_kernel, linked), grid=(n // ib,), ou...  39.1 us
    pallas_call x1, Pallas kernels, finish(): pl.pallas_call(functools.partial(finish_kernel, len(shared)), out_shape=o...  8.19 us

commit v1 on v0

--- a/solution.py
+++ b/solution.py
@@ -17,6 +17,7 @@
 TILE = 256
 D = 384
 FF = 1536
+IMAGES_AT_ONCE = 1
 VMEM = pl.BlockSpec(memory_space=pltpu.VMEM)
 
 
@@ -72,11 +73,12 @@
             z = (r // 4 + k) % 4
             self.others.append(({"h": z // 2, "l": z % 2}, (z * 4 + r % 4, y)))
 
+    def greet(self, partners):
+        for partner in partners:
+            pl.semaphore_signal(pltpu.get_barrier_semaphore(), inc=1, device_id=partner, device_id_type=MESH)
+
     def meet(self, partners):
-        barrier = pltpu.get_barrier_semaphore()
-        for partner in partners:
-            pl.semaphore_signal(barrier, inc=1, device_id=partner, device_id_type=MESH)
-        pl.semaphore_wait(barrier, len(partners))
+        pl.semaphore_wait(pltpu.get_barrier_semaphore(), len(partners))
 
 
 class Links:
@@ -102,7 +104,7 @@
 
 def fwd_kernel(linked, *refs):
     names = ["tokens", "cot", "routes", "gains", "wqkv", "wo", "win", "wout"]
-    names += ["x0", "cot_out", "x1", "x2", "x3", "qkv1", "qkv2", "o1", "o2", "p1", "p2", "u", "gp", "c"]
+    names += ["routes_out", "x0", "cot_out", "x1", "x2", "x3", "qkv1", "qkv2", "o1", "o2", "p1", "p2", "u", "gp", "c"]
     if linked:
         names += ["c_rx", "cot_rx", "routes_rx"]
     names += ["wide"]
@@ -124,23 +126,29 @@
         def exchange(at, src, dst):
             return links.copy(at, src, dst, place.partner["y"])
 
-        early = [exchange(0, r["cot_out"], r["cot_rx"]), exchange(1, r["routes"], r["routes_rx"])]
+        early = [exchange(0, r["cot_out"], r["cot_rx"]), exchange(1, r["routes_out"], r["routes_rx"])]
 
         def c_copy(image):
             return exchange(2 + image, r["c_scr"].at[image], r["c_rx"].at[image])
 
     @pl.when(step == 0)
     def _():
+        if linked:
+            place.greet([place.partner["y"]])
         wide = r["wide"]
-        for source, target in (("tokens", "x0"), ("cot", "cot_out")):
+        slots = r["routes_out"]
+        slots[...] = jnp.full(slots.shape, -1, jnp.int32)
+        for i in range(images):
+            slots[0:2, i * ROWS : i * ROWS + PATCHES] = r["routes"][:, i * PATCHES : (i + 1) * PATCHES]
+        for source, target in (("cot", "cot_out"), ("tokens", "x0")):
             wide[0 : images * PATCHES] = r[source][...].astype(F32)
             for i in range(images):
                 rows = wide[i * PATCHES : i * PATCHES + ROWS]
                 r[target][i] = jnp.where(real, rows, 0.0).astype(BF)
-        if linked:
-            place.meet([place.partner["y"]])
-            for copy in early:
-                copy.start()
+            if linked and source == "cot":
+                place.meet([place.partner["y"]])
+                for copy in early:
+                    copy.start()
 
     def attend_image(i, qkv_ref, o_ref, p_ref):
         for pair in range(HEADS // 2):
@@ -202,7 +210,7 @@
 
 def dense_forward(tokens, cot, routes, gains, wqkv, wo, win, wout, linked):
     n = tokens.shape[0] // PATCHES
-    ib = 2 if n % 2 == 0 else 1
+    ib = IMAGES_AT_ONCE if n % IMAGES_AT_ONCE == 0 else 1
 
     def out(*shape, dtype=BF):
         return jax.ShapeDtypeStruct((n,) + shape, dtype)
@@ -211,13 +219,14 @@
         return pl.BlockSpec((ib,) + tuple(shape[1:]), lambda i: (i,) + (0,) * (len(shape) - 1))
 
     whole = pl.BlockSpec((n, ROWS, D), lambda i: (0, 0, 0))
-    outs = [out(ROWS, D)] * 2 + [out(ROWS, D, dtype=F32)] * 3 + [out(ROWS, 3 * D)] * 2 + [out(ROWS, D)] * 2
+    routes_shape = jax.ShapeDtypeStruct((8, n * ROWS), jnp.int32)
+    outs = [routes_shape] + [out(ROWS, D)] * 2 + [out(ROWS, D, dtype=F32)] * 3 + [out(ROWS, 3 * D)] * 2 + [out(ROWS, D)] * 2
     outs += [out(HEADS, ROWS, ROWS)] * 2 + [out(ROWS, FF)] * 2 + [out(ROWS, D)]
-    out_specs = [whole, whole] + [block(o.shape) for o in outs[2:]]
+    out_specs = [pl.BlockSpec(routes_shape.shape, lambda i: (0, 0)), whole, whole] + [block(o.shape) for o in outs[3:]]
     scratch = [pltpu.VMEM(((n - 1) * PATCHES + ROWS, D), F32)]
     params = dict(vmem_limit_bytes=62 << 20)
     if linked:
-        outs += [out(ROWS, D)] * 2 + [jax.ShapeDtypeStruct(routes.shape, jnp.int32)]
+        outs += [out(ROWS, D)] * 2 + [routes_shape]
         out_specs += [pl.BlockSpec(memory_space=pl.ANY)] * 3
         copies = pltpu.SemaphoreType.DMA((2 + n,))
         scratch += [pltpu.VMEM((n, ROWS, D), BF), copies, copies]
@@ -359,7 +368,7 @@
 
     def tile(row, size):
         at = pl.multiple_of(begin + row, 16)
-        here = pl.ds(pl.multiple_of(row, 128), size)
+        here = pl.ds(pl.multiple_of(row, TILE // 4), size)
         lane = lax.broadcasted_iota(jnp.int32, (size, 128), 1)
         x = xg[pl.ds(at, size), 0:D]
         info = xg[pl.ds(at, size), D : D + 128].astype(F32)
@@ -383,7 +392,7 @@
         low = dg - dg.astype(BF).astype(F32)
         slots[pl.ds(at, size), 2 * D :] = jnp.where(lane == 0, dg, jnp.where(lane == 1, low, 0.0)).astype(BF)
 
-    whole = (n + TILE // 2 - 1) // TILE
+    whole = (n + TILE // 4 - 1) // TILE
 
     def full_tile(j, _):
         tile(j * TILE, TILE)
@@ -391,14 +400,16 @@
 
     lax.fori_loop(0, whole, full_tile, 0)
 
-    @pl.when(n > whole * TILE)
-    def _():
-        tile(whole * TILE, TILE // 2)
-        rest = pl.ds(pl.multiple_of(whole * TILE + TILE // 2, 128), TILE // 2)
-        for scratch in (dy_scr, u_scr, gp_scr):
-            scratch[rest] = jnp.zeros((TILE // 2,) + scratch.shape[1:], BF)
-
-    after = pl.multiple_of(begin + (n + 127) // 128 * 128, 16)
+    for size in range(TILE // 4, TILE, TILE // 4):
+
+        @pl.when((n > whole * TILE + size - TILE // 4) & (n <= whole * TILE + size))
+        def _(size=size):
+            tile(whole * TILE, size)
+            rest = pl.ds(pl.multiple_of(whole * TILE + size, TILE // 4), TILE - size)
+            for scratch in (dy_scr, u_scr, gp_scr):
+                scratch[rest] = jnp.zeros((TILE - size,) + scratch.shape[1:], BF)
+
+    after = pl.multiple_of(begin + (n + TILE // 4 - 1) // (TILE // 4) * (TILE // 4), 16)
     slots[pl.ds(after, 256)] = jnp.zeros((256, 2 * D + 128), BF)
 
     rounded = (n + TILE - 1) // TILE
@@ -677,24 +688,24 @@
         self.copy(k).start()
 
 
-GROUPS = ((48, "yxz"), (48, "xyz"), (48, "yxz"), (32, "yxz"), (16, "xyz"))
+GROUPS = ((48, "yxz"), (48, "xyz"), (48, "yxz"), (32, "yxz"), (16, "yxz"))
 GROUP_ROWS = (0, 1536, 3072, 4608, 5632)
 EXPERT_ORDERS = ("lhx", "xlh", "xlh", "xlh")
 
 ORDER = (
-    ("E", 0, 0), ("d", 0, 0), ("d", 1, 0), ("E", 1, 0), ("run", 0, 0), ("E", 1, 1), ("d", 2, 0), ("E", 2, 0),
-    ("d", 3, 0), ("E", 0, 1), ("run", 1, 0), ("y", 0, 0), ("E", 3, 0), ("run", 2, 0), ("E", 2, 1), ("run", 3, 0),
-    ("run", 4, 0), ("run", 5, 0), ("E", 1, 2), ("run", 6, 0), ("run", 7, 0), ("S", 0, 0), ("E", 0, 2), ("run", 8, 0),
-    ("E", 3, 1), ("run", 9, 0), ("run", 10, 0), ("run", 11, 0), ("run", 12, 0), ("S", 0, 1), ("S", 2, 0), ("E", 2, 2),
-    ("run", 13, 0), ("S", 1, 0), ("run", 14, 0), ("S", 1, 1), ("S", 2, 1), ("E", 1, 3), ("run", 15, 0), ("S", 0, 2),
-    ("run", 16, 0), ("E", 3, 2), ("run", 17, 0), ("S", 2, 2), ("run", 18, 0), ("S", 3, 0), ("S", 0, 3), ("S", 1, 2),
-    ("E", 1, 4), ("run", 19, 0), ("S", 2, 3), ("S", 4, 0), ("S", 3, 1), ("S", 0, 4), ("S", 4, 1), ("S", 1, 3),
-    ("S", 2, 4), ("S", 3, 2), ("S", 4, 2), ("S", 0, 5), ("S", 4, 3), ("few", 0, 0), ("S", 3, 3), ("S", 1, 4),
-    ("few", 1, 0), ("S", 0, 6), ("few", 2, 0), ("S", 2, 5), ("S", 4, 4), ("S", 3, 4), ("E", 0, 3), ("few", 3, 0),
-    ("S", 1, 5), ("S", 4, 5), ("S", 3, 5), ("S", 2, 6), ("E", 3, 3), ("run", 20, 0), ("S", 0, 7), ("S", 1, 6),
-    ("few", 4, 0), ("S", 3, 6), ("S", 4, 6), ("E", 2, 3), ("E", 3, 4), ("E", 0, 4), ("S", 1, 7), ("few", 5, 0),
-    ("S", 2, 7), ("S", 4, 7), ("S", 3, 7), ("S", 0, 8), ("S", 2, 8), ("S", 1, 8), ("S", 4, 8), ("E", 2, 4),
-    ("S", 3, 8),
+    ("E", 3, 0), ("E", 0, 0), ("d", 0, 0), ("E", 1, 0), ("E", 2, 0), ("E", 3, 1), ("d", 1, 0), ("run", 0, 0),
+    ("d", 2, 0), ("E", 0, 1), ("run", 1, 0), ("d", 3, 0), ("E", 1, 1), ("E", 2, 1), ("y", 0, 0), ("run", 2, 0),
+    ("run", 3, 0), ("E", 3, 2), ("run", 4, 0), ("run", 5, 0), ("run", 6, 0), ("S", 0, 0), ("run", 7, 0),
+    ("run", 8, 0), ("run", 9, 0), ("E", 0, 2), ("S", 0, 1), ("run", 10, 0), ("E", 1, 2), ("run", 11, 0),
+    ("run", 12, 0), ("run", 13, 0), ("S", 1, 0), ("S", 2, 0), ("run", 14, 0), ("S", 0, 2), ("run", 15, 0),
+    ("S", 2, 1), ("E", 3, 3), ("run", 16, 0), ("S", 1, 1), ("S", 0, 3), ("run", 17, 0), ("run", 18, 0), ("S", 4, 0),
+    ("S", 3, 0), ("S", 2, 2), ("run", 19, 0), ("S", 4, 1), ("S", 1, 2), ("few", 0, 0), ("S", 0, 4), ("S", 3, 1),
+    ("S", 2, 3), ("S", 4, 2), ("S", 0, 5), ("S", 4, 3), ("S", 1, 3), ("S", 3, 2), ("S", 2, 4), ("S", 0, 6),
+    ("S", 3, 3), ("S", 1, 4), ("E", 3, 4), ("few", 1, 0), ("E", 0, 3), ("S", 3, 4), ("S", 4, 4), ("S", 2, 5),
+    ("E", 2, 2), ("few", 2, 0), ("E", 1, 3), ("S", 1, 5), ("S", 3, 5), ("S", 2, 6), ("S", 4, 5), ("E", 0, 4),
+    ("few", 3, 0), ("S", 1, 6), ("run", 20, 0), ("S", 3, 6), ("S", 4, 6), ("E", 2, 3), ("S", 1, 7), ("few", 4, 0),
+    ("S", 2, 7), ("E", 1, 4), ("S", 3, 7), ("S", 0, 7), ("S", 1, 8), ("S", 4, 7), ("S", 3, 8), ("S", 2, 8),
+    ("S", 0, 8), ("E", 2, 4), ("S", 4, 8), ("few", 5, 0),
 )
 
 LOADED = ("c", "x3", "cot", "d", "delta", "x2", "qkv", "o", "p", "wo", "wqkv", "x1", "wout", "gp", "u", "win", "y", "x0")
@@ -736,7 +747,9 @@
     if linked:
         place = Place()
         links = Links(r["send"], r["recv"])
-        place.meet([place.partner[b] for b in "cyx"] + [device for _, device in place.others])
+        partners = [place.partner[b] for b in "cyx"] + [device for _, device in place.others]
+        place.greet(partners)
+        place.meet(partners)
         beside = place.partner["y"]
         delta_copy = links.copy(links.reserve(1), r["delta_send"], r["delta_rx"], beside)
         delta_copy.start()
@@ -1091,16 +1104,12 @@
     choices = routes.shape[1]
     capacity = 2 * choices * row_count // (local * groups)
     images = row_count // PATCHES
-    n_tok = images * ROWS
-    routes_t = routes.T.reshape(choices, images, PATCHES)
-    routes_t = jnp.pad(routes_t, ((0, 8 - choices), (0, 0), (0, ROWS - PATCHES)), constant_values=-1)
-    routes_t = routes_t.reshape(8, n_tok)
     router_t = router.T
     rep = lax.axis_size("rep")
     known = (rep, groups, local) == (16, 2, 4)
     owners = (2, 2, 2, 2) if known else (rep,)
-    x0, cot, x1, x2, x3, qkv1, qkv2, o1, o2, p1, p2, u, gp, c, *received = dense_forward(
-        tokens, cotangent, routes_t, norm_gains, attn_qkv, attn_out, mlp_in, mlp_out, known
+    routes_t, x0, cot, x1, x2, x3, qkv1, qkv2, o1, o2, p1, p2, u, gp, c, *received = dense_forward(
+        tokens, cotangent, routes.T, norm_gains, attn_qkv, attn_out, mlp_in, mlp_out, known
     )
 
     def of_all(mine, place):

time: 208 us -> 200 us (0.962)
  Pallas kernels: 202 us -> 197 us
    pallas_call x1, Pallas kernels: 112 us -> 106 us  [dense_backward(): pl.pallas_call(functools.partial(bwd_kernel, linked), out_shape=outs, in_...]
    pallas_call x1, Pallas kernels: 42.6 us -> 45.5 us  [experts_all(): pl.pallas_call(functools.partial(experts_kernel, groups, local, 'exp'), g...]
where the time goes in v1:
time: 200 us; the launch traced here: 198 us
  Pallas kernels  197 us (98%)
    pallas_call x1, Pallas kernels, dense_backward(): pl.pallas_call(functools.partial(bwd_kernel, linked), out_shape=outs, in_...  106 us
    pallas_call x1, Pallas kernels, experts_all(): pl.pallas_call(functools.partial(experts_kernel, groups, local, 'exp'), g...  45.5 us
    pallas_call x1, Pallas kernels, dense_forward(): pl.pallas_call(functools.partial(fwd_kernel, linked), grid=(n // ib,), ou...  37.6 us
    pallas_call x1, Pallas kernels, finish(): pl.pallas_call(functools.partial(finish_kernel, len(shared)), out_shape=o...  8.19 us

profile of v1, /device:TPU:0, one launch (start us, length us, event | category | flops | bytes accessed | tf_op | source)
XLA Modules:
  0.0 198.1 jit_solution(6758592419923436484)
XLA Ops:
  0.6 37.6 %dense_forward.1 = (s32[8,832]{1,0:T(8,128)}, bf16[4,208,384]{2,1,0:T(8,128)(2,1)}, bf16[4,208,384]{2,1,0:T(8,128)(2,1)}, f32[4,208,384]{2,1,0:T(8,128)}, f32[4,...) custom-call(bf16[788,384]{1,0:T(8,128)(2,1)} %refs_0_.2, ...), custom_call_target="tpu_custom_call" | custom-call | tf_op jit(solution)/shard_map/dense_forward/pallas_call | solution.py:234
  38.3 45.5 %experts.1 = (bf16[4,2,1536,384]{3,2,1,0:T(8,128)(2,1)}, bf16[832,384]{1,0:T(8,128)(2,1)}, bf16[832,384]{1,0:T(8,128)(2,1)}, bf16[832,384]{1,0:T(8,128)(2,1)}, b...) custom-call(bf16[832,384]{1,0:T(8,128)(2,1)} %bitcast.20, bf16[832,384]{1,0:T(8,128)(2,1)} %bitcast.29, ...), custom_call_target="tpu_custom_call" | custom-call | tf_op jit(solution)/shard_map/experts/pallas_call | solution.py:512
  83.8 105.9 %dense_backward.1 = (bf16[4,208,384]{2,1,0:T(8,128)(2,1)}, f32[4,208,384]{2,1,0:T(8,128)}, f32[16,384]{1,0:T(8,128)}, f32[4,2,96,384]{3,2,1,0:T(8,128)}, bf16[2,...) custom-call(f32[4,384]{1,0:T(4,128)} %refs_0_.3, ...), custom_call_target="tpu_custom_call" | custom-call | tf_op jit(solution)/shard_map/dense_backward/pallas_call | solution.py:997
  189.7 8.2 %finish.1 = (bf16[788,384]{1,0:T(8,128)(2,1)}, f32[788,384]{1,0:T(8,128)}, f32[2,384,1152]{2,1,0:T(8,128)}, f32[2,384,384]{2,1,0:T(8,128)}, f32[4,384]{1,0:T(4,1...) custom-call(bf16[4,208,384]{2,1,0:T(8,128)(2,1)} %get-tuple-element., ...), custom_call_target="tpu_custom_call" | custom-call | tf_op jit(solution)/shard_map/finish/pallas_call | solution.py:1076

commit v2 on v1

--- a/solution.py
+++ b/solution.py
@@ -103,11 +103,12 @@
 
 
 def fwd_kernel(linked, *refs):
-    names = ["tokens", "cot", "routes", "gains", "wqkv", "wo", "win", "wout"]
+    weights = ["wqkv", "wo", "win", "wout"]
+    names = ["tokens", "cot", "routes", "gains"] + ["far_" + name for name in weights]
     names += ["routes_out", "x0", "cot_out", "x1", "x2", "x3", "qkv1", "qkv2", "o1", "o2", "p1", "p2", "u", "gp", "c"]
     if linked:
         names += ["c_rx", "cot_rx", "routes_rx"]
-    names += ["wide"]
+    names += ["wide"] + weights + ["sem"]
     if linked:
         names += ["c_scr", "send", "recv"]
     r = dict(zip(names, refs, strict=True))
@@ -135,6 +136,9 @@
     def _():
         if linked:
             place.greet([place.partner["y"]])
+        loads = [pltpu.make_async_copy(r["far_" + w], r[w], r["sem"].at[k]) for k, w in enumerate(weights)]
+        for load in loads:
+            load.start()
         wide = r["wide"]
         slots = r["routes_out"]
         slots[...] = jnp.full(slots.shape, -1, jnp.int32)
@@ -149,6 +153,8 @@
                 place.meet([place.partner["y"]])
                 for copy in early:
                     copy.start()
+        for load in loads:
+            load.wait()
 
     def attend_image(i, qkv_ref, o_ref, p_ref):
         for pair in range(HEADS // 2):
@@ -224,6 +230,7 @@
     outs += [out(HEADS, ROWS, ROWS)] * 2 + [out(ROWS, FF)] * 2 + [out(ROWS, D)]
     out_specs = [pl.BlockSpec(routes_shape.shape, lambda i: (0, 0)), whole, whole] + [block(o.shape) for o in outs[3:]]
     scratch = [pltpu.VMEM(((n - 1) * PATCHES + ROWS, D), F32)]
+    scratch += [pltpu.VMEM(w.shape, BF) for w in (wqkv, wo, win, wout)] + [pltpu.SemaphoreType.DMA((4,))]
     params = dict(vmem_limit_bytes=62 << 20)
     if linked:
         outs += [out(ROWS, D)] * 2 + [routes_shape]
@@ -235,7 +242,7 @@
         functools.partial(fwd_kernel, linked),
         grid=(n // ib,),
         out_shape=outs,
-        in_specs=[VMEM] * 8,
+        in_specs=[VMEM] * 4 + [pl.BlockSpec(memory_space=pl.ANY)] * 4,
         out_specs=out_specs,
         scratch_shapes=scratch,
         compiler_params=pltpu.CompilerParams(**params),
@@ -709,6 +716,7 @@
 )
 
 LOADED = ("c", "x3", "cot", "d", "delta", "x2", "qkv", "o", "p", "wo", "wqkv", "x1", "wout", "gp", "u", "win", "y", "x0")
+EARLY = 10
 
 
 def bwd_kernel(linked, *refs):
@@ -722,6 +730,9 @@
     else:
         names += ["shared_out"]
     names += ["v_" + n for n in LOADED] + ["gv", "a_scr", "dbr_scr", "dqkv_scr", "sem"]
+    names += ["v_act", "v_gin", "leave_sem"]
+    if linked:
+        names += ["v_eg"] + ["v_out" + str(g) for g in range(len(GROUPS))]
     if linked:
         names += ["d_rx", "delta_rx", "y_rx", "own", "part", "small_src", "small_rx", "eg_sem", "send", "recv"]
         names += ["src" + str(g) for g in range(len(GROUPS))]
@@ -744,6 +755,12 @@
         for name in wanted:
             copies[name].wait()
 
+    leaving = []
+
+    def leave(source, target):
+        leaving.append(pltpu.make_async_copy(source, target, r["leave_sem"].at[len(leaving)]))
+        leaving[-1].start()
+
     if linked:
         place = Place()
         links = Links(r["send"], r["recv"])
@@ -762,7 +779,7 @@
         experts = [
             ExpertSum(
                 place, links, j, turn.index(j) % 2, r["eg"], r["own"], r["part"], [r["erx" + str(j) + str(k)] for k in range(3)],
-                order, r["eg_out"], r["eg_sem"],
+                order, r["v_eg"], r["eg_sem"],
             )
             for j, order in enumerate(EXPERT_ORDERS)
         ]
@@ -772,13 +789,13 @@
         sums = []
         for g, (_, order) in enumerate(GROUPS):
             rx = [r["rx" + str(g) + str(k)] for k in range(len(order) + 1)]
-            sums.append(SharedSum(place, links, r["src" + str(g)], rx[0], rx[1:], order, r["out" + str(g)]))
+            sums.append(SharedSum(place, links, r["src" + str(g)], rx[0], rx[1:], order, r["v_out" + str(g)]))
         few = SmallSum(place, links, r["small_src"], r["small_rx"])
         small = r["small_src"].at[0]
         small[...] = jnp.zeros(small.shape, F32)
     else:
         small = r["small_out"]
-    for name in LOADED:
+    for name in LOADED[:EARLY]:
         fetch(name, second.get(name, name))
 
     def keep(block, value):
@@ -823,6 +840,8 @@
         add_gain(3, by_gain)
         if i == 0:
             need("x2", "qkv", "o", "p", "wo")
+            for name in LOADED[EARLY:]:
+                fetch(name, name)
         attend_image(i, 1, gains[2:3], r["v_x2"])
 
     def attend_image(i, layer, gain, x):
@@ -909,7 +928,8 @@
         attend_image(i, 0, gains[0:1], r["v_x0"])
 
     def last_close():
-        close(r["v_x0"], 0, 0, r["gin_out"])
+        close(r["v_x0"], 0, 0, r["v_gin"])
+        leave(r["v_gin"], r["gin_out"])
 
     def act():
         need("y")
@@ -919,7 +939,8 @@
             x4 = r["v_x3"][i] + r["v_y"][i].astype(F32)
             if linked:
                 x4 = x4 + r["y_rx"][i].astype(F32)
-            r["act_out"][i] = x4.astype(BF)
+            r["v_act"][i] = x4.astype(BF)
+        leave(r["v_act"], r["act_out"])
 
     compute = [router] + [functools.partial(first, i) for i in range(images)]
     compute += [lambda: attend_weights(0), first_close] + [functools.partial(mlp, i) for i in range(images)]
@@ -928,6 +949,8 @@
     if not linked:
         for step in compute:
             step()
+        for copy in leaving:
+            copy.wait()
         return
     done = 0
     for kind, at, what in ORDER:
@@ -942,10 +965,16 @@
             few.run(at, r["small_out"])
         elif kind == "E":
             experts[at].run(what)
+            if what == 4:
+                leave(r["v_eg"].at[at], r["eg_out"].at[at])
             if what == 1 and turn.index(at) + 2 < len(turn):
                 experts[turn[turn.index(at) + 2]].load.start()
         else:
             sums[at].run(what)
+            if what == 2 * len(GROUPS[at][1]) + 2:
+                leave(r["v_out" + str(at)], r["out" + str(at)])
+    for copy in leaving:
+        copy.wait()
 
 
 def dense_backward(weights, router_t, routes, saved, cot, d, delta, y, sent=None):
@@ -970,6 +999,8 @@
     scratch = [vm(loaded[name].shape, loaded[name].dtype) for name in LOADED]
     scratch += [vm((images, ROWS, D), F32), vm((images, ROWS, D), BF), vm((images, ROWS, D), BF)]
     scratch += [vm((images, ROWS, 3 * D), BF), pltpu.SemaphoreType.DMA((len(LOADED),))]
+    leavers = 2 + (sent[-1].shape[0] + len(GROUPS) if linked else 0)
+    scratch += [vm((images, ROWS, D), BF), vm((images, ROWS, D), F32), pltpu.SemaphoreType.DMA((leavers,))]
     params = dict(vmem_limit_bytes=62 << 20)
     if linked:
         eg = sent[-1]
@@ -977,6 +1008,7 @@
         outs.append(jax.ShapeDtypeStruct((local, 2, share, D), F32))
         outs += [jax.ShapeDtypeStruct((2,) * 5 + (rows, D), BF) for rows, _ in GROUPS]
         copies = 2 + images + 4 * local + 15 * len(GROUPS) + len(BITS)
+        scratch += [vm((local, 2, share, D), F32)] + [vm((2,) * 5 + (rows, D), BF) for rows, _ in GROUPS]
         scratch += [vm(d.shape, BF), vm(delta.shape, F32), vm(y.shape, BF)]
         scratch += [
             vm((2, 2, 2, 2, 2, share, D), BF),
@@ -994,11 +1026,13 @@
                 scratch.append(vm((3, rows, D), BF))
         scratch += [vm((2,) * (3 - k) + (share, D), BF) for _ in EXPERT_ORDERS for k in range(3)]
         params.update(collective_id=1, has_side_effects=True)
+    far = pl.BlockSpec(memory_space=pl.ANY)
+    out_specs = [far, far, VMEM] + [far if linked else VMEM] * (len(outs) - 3)
     return pl.pallas_call(
         functools.partial(bwd_kernel, linked),
         out_shape=outs,
         in_specs=[VMEM] * 3 + [pl.BlockSpec(memory_space=pl.ANY)] * (len(ins) - 3),
-        out_specs=[VMEM] * len(outs),
+        out_specs=out_specs,
         scratch_shapes=scratch,
         compiler_params=pltpu.CompilerParams(**params),
         name="dense_backward",

time: 200 us -> 196 us (0.980)
  Pallas kernels: 197 us -> 192 us
    pallas_call x1, Pallas kernels: 45.5 us -> 35.6 us  [experts_all(): pl.pallas_call(functools.partial(experts_kernel, groups, local, 'exp'), g...]
    pallas_call x1, Pallas kernels: 106 us -> 112 us  [dense_backward(): pl.pallas_call(functools.partial(bwd_kernel, linked), out_shape=outs, in_...]
where the time goes in v2:
time: 196 us; the launch traced here: 193 us
  Pallas kernels  192 us (98%)
    pallas_call x1, Pallas kernels, dense_backward(): pl.pallas_call(functools.partial(bwd_kernel, linked), out_shape=outs, in_...  112 us
    pallas_call x1, Pallas kernels, dense_forward(): pl.pallas_call(functools.partial(fwd_kernel, linked), grid=(n // ib,), ou...  36.2 us
    pallas_call x1, Pallas kernels, experts_all(): pl.pallas_call(functools.partial(experts_kernel, groups, local, 'exp'), g...  35.6 us
    pallas_call x1, Pallas kernels, finish(): pl.pallas_call(functools.partial(finish_kernel, len(shared)), out_shape=o...  8.19 us

profile of v2, /device:TPU:0, one launch (start us, length us, event | category | flops | bytes accessed | tf_op | source)
XLA Modules:
  0.0 192.8 jit_solution(5749708918996159199)
XLA Ops:
  0.6 36.2 %dense_forward.1 = (s32[8,832]{1,0:T(8,128)}, bf16[4,208,384]{2,1,0:T(8,128)(2,1)}, bf16[4,208,384]{2,1,0:T(8,128)(2,1)}, f32[4,208,384]{2,1,0:T(8,128)}, f32[4,...) custom-call(bf16[788,384]{1,0:T(8,128)(2,1)} %refs_0_.2, ...), custom_call_target="tpu_custom_call" | custom-call | tf_op jit(solution)/shard_map/dense_forward/pallas_call | solution.py:241
  36.8 35.6 %experts.1 = (bf16[4,2,1536,384]{3,2,1,0:T(8,128)(2,1)}, bf16[832,384]{1,0:T(8,128)(2,1)}, bf16[832,384]{1,0:T(8,128)(2,1)}, bf16[832,384]{1,0:T(8,128)(2,1)}, b...) custom-call(bf16[832,384]{1,0:T(8,128)(2,1)} %bitcast.20, bf16[832,384]{1,0:T(8,128)(2,1)} %bitcast.29, ...), custom_call_target="tpu_custom_call" | custom-call | tf_op jit(solution)/shard_map/experts/pallas_call | solution.py:519
  72.4 112.0 %dense_backward.1 = (bf16[4,208,384]{2,1,0:T(8,128)(2,1)}, f32[4,208,384]{2,1,0:T(8,128)}, f32[16,384]{1,0:T(8,128)}, f32[4,2,96,384]{3,2,1,0:T(8,128)}, bf16[2,...) custom-call(f32[4,384]{1,0:T(4,128)} %refs_0_.3, ...), custom_call_target="tpu_custom_call" | custom-call | tf_op jit(solution)/shard_map/dense_backward/pallas_call | solution.py:1031
  184.4 8.2 %finish.1 = (bf16[788,384]{1,0:T(8,128)(2,1)}, f32[788,384]{1,0:T(8,128)}, f32[2,384,1152]{2,1,0:T(8,128)}, f32[2,384,384]{2,1,0:T(8,128)}, f32[4,384]{1,0:T(4,1...) custom-call(bf16[4,208,384]{2,1,0:T(8,128)(2,1)} %get-tuple-element., ...), custom_call_target="tpu_custom_call" | custom-call | tf_op jit(solution)/shard_map/finish/pallas_call | solution.py:1110
